TPU v7x, 32 devices: a whole 2x2x4 slice. The times are simulated.
32 devices in a mesh: angle: 8 (over y, x, core), frame: 4 (over z).
Axes of the slice: x: 2, y: 2, z: 4, core: 2. Of those that a mesh axis runs over, the one named last changes fastest.
Arguments:
- volume: float32 [32, 8192], P('frame', 'angle'), may hold values from -6 to 6
- measured: bfloat16 [8, 32, 12288], P(None, 'frame', 'angle'), may hold values from -6 to 6
- tiles: bfloat16 [8, 1024, 1536], replicated, may hold values from -0.0625 to 0.0625
- tile_index: int32 [8, 8], replicated, may hold values from 0 to 7, as said below
- warp_coef: bfloat16 [8, 3, 32, 8192], P(None, None, 'frame', 'angle'), may hold values from 0.099609375 to 0.59765625
- warp_offset: int32 [8, 32], P(None, 'frame'), may hold values from -2 to 0
- ray_weight: float32 [32, 12288], P('frame', 'angle'), may hold values from 0.5 to 2
- redundancy: float32 [12288], P('angle'), may hold values from 0.2 to 0.8
- conj_view: int32 [8, 2], P('angle'), may hold values from 0 to 1, as said below
- voxel_weight: float32 [32, 8192], P('frame', 'angle'), may hold values from 0.05 to 0.2
Outputs:
- volume_next: float32 [32, 8192], P('frame', 'angle')
- weighted: bfloat16 [8, 32, 12288], P(None, 'frame', 'angle')
Inputs may be any that keep to these rules, and one draw needn't show every extreme that they name: `conj_view`: each row is a permutation of 0..1, and row b + 4 is the inverse permutation of row b for b < 4. `tile_index`: every row is a permutation of 0..7.
All inputs are finite; a program needn't handle non-finite values.
Results may differ from a plain program's by a relative error of at most 0.0034.
Values may be sent and summed in bfloat16 or wider, within the bound.
A program may use at most 256 MiB of HBM per device.

v0:
```python
import jax
import jax.numpy as jnp
from jax import lax
from jax.sharding import PartitionSpec as P

VB = 2
UW = 768
HALO = 2


def extended_2(value, sides, width):
    for axis, dim in sides:
        devices, length = (lax.axis_size(axis), value.shape[dim])
        up = [(i, (i + 1) % devices) for i in range(devices - 1)]
        down = [(j, i) for i, j in up]
        last = lax.slice_in_dim(value, length - width, length, axis=dim)
        leading = lax.slice_in_dim(value, 0, width, axis=dim)
        before = lax.ppermute(last, axis, up)
        after = lax.ppermute(leading, axis, down)
        value = jnp.concatenate([before, value, after], axis=dim)
    return value


def shifted(block, axis, distance):
    devices = range(lax.axis_size(axis))
    route = [((i - distance) % len(devices), i) for i in devices]
    return lax.ppermute(block, axis, route)


def warp_weights(offsets, coefs, distance):
    weights = jnp.zeros(coefs[:, 0].shape, jnp.float32)
    for tap_index in range(coefs.shape[1]):
        selected = (offsets + tap_index == distance).astype(jnp.float32)[:, :, None]
        weights = weights + selected * coefs[:, tap_index].astype(jnp.float32)
    return weights


def source_terms(offsets, coefs, images, distance):
    return jnp.sum(warp_weights(offsets, coefs, distance) * images, axis=0)


def body(
    volume,
    measured,
    tiles,
    tile_index,
    warp_coef,
    warp_offset,
    ray_weight,
    redundancy,
    conj_view,
    voxel_weight,
):
    frames, slab_rows, rays = measured.shape
    sector = volume.shape[1]
    stacked = frames * slab_rows
    sector_total = lax.axis_size("angle")
    position = lax.axis_index("angle")
    sector_ids = lax.dynamic_index_in_dim(tile_index, position, 1, False)
    block_ids = lax.dynamic_index_in_dim(tile_index, position, 0, False)
    extended = extended_2(volume, (("frame", 0),), HALO)
    warped = jnp.zeros((frames, slab_rows, sector), jnp.float32)
    for distance in range(-HALO, HALO + 1):
        source_rows = extended[HALO + distance : HALO + distance + slab_rows]
        warped = warped + warp_weights(warp_offset, warp_coef, distance) * source_rows[None]
    warped = warped.astype(jnp.bfloat16).reshape(stacked, sector)
    shard_piece = lax.all_gather(warped, "angle", axis=1, tiled=True)
    count = shard_piece.shape[1] // sector
    chosen = block_ids
    footprints = jnp.take(tiles, chosen, axis=0)
    pieces = shard_piece.reshape(stacked, count, sector)
    projected = jnp.einsum("mnj,njr->mr", pieces, footprints, preferred_element_type=jnp.float32)
    residual = measured.astype(jnp.float32) - projected.reshape(frames, slab_rows, rays)
    partner = shifted(residual, "angle", sector_total // 2)
    partner = partner.reshape(frames, slab_rows, VB, UW)
    mirrored = jnp.take(partner, conj_view[0], axis=2)[..., ::-1].reshape(frames, slab_rows, rays)
    weighted = ((redundancy * residual + (1.0 - redundancy) * mirrored) * ray_weight[None]).astype(
        jnp.bfloat16
    )
    ray_rows = weighted.reshape(stacked, rays)
    shard_piece = lax.all_gather(ray_rows, "angle", axis=1, tiled=True)
    count = shard_piece.shape[1] // rays
    chosen = sector_ids
    footprints = jnp.take(tiles, chosen, axis=0)
    pieces = shard_piece.reshape(stacked, count, rays)
    image = jnp.einsum("mnr,njr->mj", pieces, footprints, preferred_element_type=jnp.float32)
    images = image.reshape(frames, slab_rows, sector)
    image_ext = extended_2(images.astype(jnp.bfloat16), (("frame", 1),), HALO).astype(images.dtype)
    coef_ext = extended_2(warp_coef, (("frame", 2),), HALO)
    offset_ext = extended_2(warp_offset, (("frame", 1),), HALO)
    gathered = jnp.zeros((slab_rows, sector), jnp.float32)
    for distance in range(-HALO, HALO + 1):
        terms = source_terms(offset_ext, coef_ext, image_ext, distance)
        gathered = gathered + terms[HALO - distance : HALO - distance + slab_rows]
    volume_next = volume + voxel_weight * gathered
    return (volume_next, weighted)


def solution(mesh):
    placed = (
        P("frame", "angle"),
        P(None, "frame", "angle"),
        P(),
        P(),
        P(None, None, "frame", "angle"),
        P(None, "frame"),
        P("frame", "angle"),
        P("angle"),
        P("angle", None),
        P("frame", "angle"),
    )
    return jax.shard_map(
        body,
        mesh=mesh,
        in_specs=placed,
        out_specs=(P("frame", "angle"), P(None, "frame", "angle")),
        check_vma=False,
    )
```

profile of v0, /device:TPU:0, one launch (start us, length us, event | category | flops | bytes accessed | tf_op | source)
XLA Modules:
  0.0 151.1 jit_solution(6929378120450286384)
XLA Ops:
  7.2 0.0 all-gather.3.cloned.1.call-start
  7.2 0.8 fusion.70
  8.1 4.9 %collective-permute-start.4 = (f32[2,1024]{1,0:T(2,128)S(1)}, f32[2,1024]{1,0:T(2,128)S(1)}, u32[]{:S(2)}, u32[]{:S(2)}) collective-permute-start(f32[2,1024]{1,0:T(2,128)S(1)} %get-tuple-element.22), channel_id=1, source_target_pairs={{0,1},{1,2},{2,3},{4,5},{5,6},{6,7},{8,9},{9,10},{10,11},{12,13},{... | collective-permute-start | bytes 24584 | tf_op jit(solution)/shard_map/ppermute | solution.py:18
  13.0 1.3 collective-permute-start.5
  14.3 0.7 compare_convert_fusion.26
  15.0 0.7 compare_and_fusion.1
  15.7 0.1 reshape.432
  15.8 0.1 reshape.434
  15.8 0.1 reshape.436
  15.9 0.1 reshape.438
  16.0 0.1 reshape.439
  16.1 0.1 reshape.440
  16.2 0.1 reshape.441
  16.2 0.1 reshape.442
  16.3 0.1 reshape.443
  16.4 0.1 reshape.444
  16.5 0.1 reshape.445
  16.6 0.1 reshape.446
  16.6 0.1 reshape.447
  16.7 0.1 reshape.448
  16.8 0.1 reshape.449
  16.9 0.0 collective-permute-done.4
  16.9 0.9 fusion.58
  17.8 0.7 collective-permute-done.5
  18.5 2.1 %fusion.45 = bf16[64,1024]{1,0:T(8,128)(2,1)} fusion(f32[8,1024]{1,0:T(8,128)S(1)} %get-tuple-element.18, f32[64]{0:T(128)S(1)} %reshape.449, f32[64]{0:T(128)S(1)} %reshape.448, f32[64]{0:T(128)S(1)} %reshape.447, f32[8,1024]{1,0:T(8,128)S(1)} %get-tuple-element.17, f32[64]{0:T(128)S(1)} %reshape.446, f32[64]{0:T(128)S(1)} %reshape.445, ...), kind=kLoop, calls=%fused_computation.80 | loop fusion | flops 2490368 | bytes 691968 | tf_op jit(solution)/shard_map/convert_element_type | solution.py:66
  20.7 0.0 all-gather.3.cloned.1.call-update
  20.7 0.0 all-gather.5.cloned.1.call-start
  20.8 17.3 %fusion.66 = (bf16[8,1024,768]{2,1,0:T(8,128)(2,1)}, bf16[8,1024,768]{2,1,0:T(8,128)(2,1)}) fusion(bf16[8,1024,1536]{2,1,0:T(8,128)(2,1)} %param.14), kind=kLoop, calls=%fused_computation.157 | loop fusion | bytes 50331648 | tf_op jit(solution)/shard_map/jit(_take)/gather | solution.py:70
  38.0 11.1 %gather_fusion.1 = bf16[8,1024,768]{2,1,0:T(8,128)(2,1)} fusion(bf16[8,1024,768]{2,1,0:T(8,128)(2,1)} %get-tuple-element.11, s32[1024]{0:T(1024)S(1)} %pad_clamp_fusion.2), kind=kCustom, calls=%fused_computation.clone | custom fusion | bytes 25165856 | tf_op jit(solution)/shard_map/jit(_take)/gather | solution.py:70
  49.1 11.1 %gather_fusion.2 = bf16[8,1024,768]{2,1,0:T(8,128)(2,1)} fusion(bf16[8,1024,768]{2,1,0:T(8,128)(2,1)} %get-tuple-element.12, s32[1024]{0:T(1024)S(1)} %pad_clamp_fusion.2), kind=kCustom, calls=%fused_computation.1.clone | custom fusion | bytes 25165856 | tf_op jit(solution)/shard_map/jit(_take)/gather | solution.py:70
  60.2 0.0 all-gather.3.cloned.1.call-done
  60.2 1.8 %copy.31 = bf16[8,8,8,1024]{3,2,1,0:T(8,128)(2,1)S(1)} copy(bf16[8,8,8,1024]{3,1,2,0:T(8,128)(2,1)} %bitcast.107) | data formatting | bytes 2097152
  62.1 0.0 copy-start.4
  62.1 0.0 copy-start.3
  62.1 0.0 copy-start.6
  62.1 10.8 %fusion.13 = f32[8,8,1536]{2,1,0:T(8,128)S(1)} fusion(bf16[8,1024,768]{2,1,0:T(8,128)(2,1)} %gather_fusion.2, bf16[8,1024,768]{2,1,0:T(8,128)(2,1)} %gather_fusion.1, pred[8]{0:T(512)(128)(4,1)S(1)} %get-tuple-element.9, bf16[8,8,1024,8]{2,3,1,0:T(8,128)(2,1)S(1)} %bitcast.108, bf16[8,8,1536]{2,1,0:T(8,128)(2,1)S(1)} %copy-done.7), kind=kOutput, calls=%fused_computation.16 | convolution fusion | flops 1673723904 | bytes 26804232 | tf_op jit(solution)/shard_map/mnj,njr->mr/dot_general | solution.py:72
  73.0 1.6 %collective-permute-start.6 = (f32[8,8,1536]{2,1,0:T(8,128)S(1)}, f32[8,8,1536]{2,1,0:T(8,128)S(1)}, u32[]{:S(2)}, u32[]{:S(2)}) collective-permute-start(f32[8,8,1536]{2,1,0:T(8,128)S(1)} %fusion.13), channel_id=1, source_target_pairs={{16,0},{20,4},{24,8},{28,12},{0,16},{4,20},{8,24},{12,28},{17,1},{... | collective-permute-start | bytes 1179656 | tf_op jit(solution)/shard_map/ppermute | solution.py:27
  74.6 8.4 %collective-permute-done.6 = f32[8,8,1536]{2,1,0:T(8,128)S(1)} collective-permute-done((f32[8,8,1536]{2,1,0:T(8,128)S(1)}, f32[8,8,1536]{2,1,0:T(8,128)S(1)}, u32[]{:S(2)}, u32[]{:S(2)}) %collective-permute-start.6) | collective-permute-done | bytes 393248 | tf_op jit(solution)/shard_map/ppermute | solution.py:27
  83.0 0.6 gather_fusion
  83.5 0.1 select_bitcast_fusion
  83.6 0.6 rev.3
  84.2 0.8 multiply_convert_fusion
  85.0 0.0 all-gather.5.cloned.1.call-update
  85.0 0.1 fusion.71
  85.1 4.2 %collective-permute-start = (s32[8,2]{1,0:T(8,128)S(1)}, s32[8,2]{1,0:T(8,128)S(1)}, u32[]{:S(2)}, u32[]{:S(2)}) collective-permute-start(s32[8,2]{1,0:T(8,128)S(1)} %get-tuple-element.53), channel_id=1, source_target_pairs={{0,1},{1,2},{2,3},{4,5},{5,6},{6,7},{8,9},{9,10},{10,11},{12,13},{... | collective-permute-start | bytes 200 | tf_op jit(solution)/shard_map/ppermute | solution.py:18
  89.3 1.3 collective-permute-start.1
  90.6 0.1 fusion.67
  90.8 4.6 %collective-permute-start.2 = (bf16[8,3,2,1024]{3,2,0,1:T(2,128)(2,1)S(1)}, bf16[8,3,2,1024]{3,2,0,1:T(2,128)(2,1)S(1)}, u32[]{:S(2)}, u32[]{:S(2)}) collective-permute-start(bf16[8,3,2,1024]{3,2,0,1:T(2,128)(2,1)S(1)} %get-tuple-element.13), channel_id=1, source_target_pairs={{0,1},{1,2},{2,3},{4,5},{5,6},{6,7},{8,9},{9,10},{10,11},{12,13},{... | collective-permute-start | bytes 294920 | tf_op jit(solution)/shard_map/ppermute | solution.py:18
  95.3 1.3 collective-permute-start.3
  96.6 0.2 dynamic-slice_reduce_fusion
  96.8 11.2 %gather_fusion.3 = bf16[8,1024,768]{2,1,0:T(8,128)(2,1)} fusion(bf16[8,1024,768]{2,1,0:T(8,128)(2,1)} %get-tuple-element.11, s32[1024]{0:T(1024)S(1)} %pad_clamp_fusion), kind=kCustom, calls=%fused_computation.2.clone | custom fusion | bytes 25165856 | tf_op jit(solution)/shard_map/jit(_take)/gather | solution.py:84
  108.1 11.1 %gather_fusion.4 = bf16[8,1024,768]{2,1,0:T(8,128)(2,1)} fusion(bf16[8,1024,768]{2,1,0:T(8,128)(2,1)} %get-tuple-element.12, s32[1024]{0:T(1024)S(1)} %pad_clamp_fusion), kind=kCustom, calls=%fused_computation.3.clone | custom fusion | bytes 25165856 | tf_op jit(solution)/shard_map/jit(_take)/gather | solution.py:84
  119.2 0.1 compare_convert_fusion.8
  119.3 0.0 all-gather.5.cloned.1.call-done
  119.3 0.0 copy-start.5
  119.3 12.6 %fusion.19 = bf16[8,8,1024]{2,1,0:T(8,128)(2,1)S(1)} fusion(bf16[8,8,8,1536]{3,1,2,0:T(8,128)(2,1)} %bitcast.111, bf16[8,1024,768]{2,1,0:T(8,128)(2,1)} %gather_fusion.4, bf16[8,1024,768]{2,1,0:T(8,128)(2,1)} %gather_fusion.3, pred[8]{0:T(512)(128)(4,1)S(1)} %compare_and_fusion), kind=kOutput, calls=%fused_computation.18 | convolution fusion | flops 1673592832 | bytes 26869768 | tf_op jit(solution)/shard_map/mnr,njr->mj/dot_general | solution.py:86
  132.0 4.4 %collective-permute-start.7 = (bf16[8,2,1024]{2,1,0:T(2,128)(2,1)S(1)}, bf16[8,2,1024]{2,1,0:T(2,128)(2,1)S(1)}, u32[]{:S(2)}, u32[]{:S(2)}) collective-permute-start(bf16[8,2,1024]{2,1,0:T(2,128)(2,1)S(1)} %get-tuple-element.15), channel_id=1, source_target_pairs={{0,1},{1,2},{2,3},{4,5},{5,6},{6,7},{8,9},{9,10},{10,11},{12,13},{... | collective-permute-start | bytes 98312 | tf_op jit(solution)/shard_map/ppermute | solution.py:18
  136.4 1.3 collective-permute-start.8
  137.8 0.4 pad_maximum_fusion
  138.2 4.1 %collective-permute-done.8 = bf16[8,2,1024]{2,1,0:T(2,128)(2,1)S(1)} collective-permute-done((bf16[8,2,1024]{2,1,0:T(2,128)(2,1)S(1)}, bf16[8,2,1024]{2,1,0:T(2,128)(2,1)S(1)}, u32[]{:S(2)}, u32[]{:S(2)}) %collective-permute-start.8) | collective-permute-done | bytes 32800 | tf_op jit(solution)/shard_map/ppermute | solution.py:19
  142.2 0.3 fusion.27
  142.6 0.5 fusion.23
  143.1 0.5 fusion.24
  143.7 0.6 fusion.60
  (32 shorter events, 0.2 us)
Async XLA Ops:
  7.2 53.1 %all-gather.3.cloned.1.call-start = ((), (), s32[]{:S(2)}) async-start(), calls=%async_computation | async-start | bytes 1179648 | tf_op jit(solution)/shard_map/all_gather | solution.py:67
  8.1 8.8 %collective-permute-start.4 = (f32[2,1024]{1,0:T(2,128)S(1)}, f32[2,1024]{1,0:T(2,128)S(1)}, u32[]{:S(2)}, u32[]{:S(2)}) collective-permute-start(f32[2,1024]{1,0:T(2,128)S(1)} %get-tuple-element.22), channel_id=1, source_target_pairs={{0,1},{1,2},{2,3},{4,5},{5,6},{6,7},{8,9},{9,10},{10,11},{12,13},{... | collective-permute-start | bytes 24584 | tf_op jit(solution)/shard_map/ppermute | solution.py:18
  13.0 5.5 %collective-permute-start.5 = (f32[2,1024]{1,0:T(2,128)S(1)}, f32[2,1024]{1,0:T(2,128)S(1)}, u32[]{:S(2)}, u32[]{:S(2)}) collective-permute-start(f32[2,1024]{1,0:T(2,128)S(1)} %get-tuple-element.23), channel_id=1, source_target_pairs={{1,0},{2,1},{3,2},{5,4},{6,5},{7,6},{9,8},{10,9},{11,10},{13,12},{... | collective-permute-start | bytes 24584 | tf_op jit(solution)/shard_map/ppermute | solution.py:19
  20.7 98.6 %all-gather.5.cloned.1.call-start = ((), (), s32[]{:S(2)}) async-start(), calls=%async_computation.1 | async-start | bytes 1769472 | tf_op jit(solution)/shard_map/all_gather | solution.py:81
  49.1 11.1 %copy-start.8 = (s32[1,2]{1,0:T(1,128)S(1)}, s32[1,2]{1,0:T(1,128)}, u32[]{:S(2)}) copy-start(s32[1,2]{1,0:T(1,128)} %param.20) | copy-start | bytes 28
  49.1 13.0 %copy-start.7 = (bf16[8,8,1536]{2,1,0:T(8,128)(2,1)S(1)}, bf16[8,8,1536]{2,1,0:T(8,128)(2,1)}, u32[]{:S(2)}) copy-start(bf16[8,8,1536]{2,1,0:T(8,128)(2,1)} %param.13) | copy-start | bytes 589828
  62.1 12.5 %copy-start.4 = (f32[1536]{0:T(1024)S(1)}, f32[1536]{0:T(1024)}, u32[]{:S(2)}) copy-start(f32[1536]{0:T(1024)} %param.19) | copy-start | bytes 18436
  62.1 22.1 %copy-start.3 = (f32[8,1536]{1,0:T(8,128)S(1)}, f32[8,1536]{1,0:T(8,128)}, u32[]{:S(2)}) copy-start(f32[8,1536]{1,0:T(8,128)} %param.18) | copy-start | bytes 147460
  62.1 22.9 %copy-start.2 = (s32[8,8]{1,0:T(8,128)S(1)}, s32[8,8]{1,0:T(8,128)}, u32[]{:S(2)}) copy-start(s32[8,8]{1,0:T(8,128)} %param.17) | copy-start | bytes 772
  62.1 28.5 %copy-start = (bf16[8,3,8,1024]{3,2,1,0:T(8,128)(2,1)S(1)}, bf16[8,3,8,1024]{3,2,1,0:T(8,128)(2,1)}, u32[]{:S(2)}) copy-start(bf16[8,3,8,1024]{3,2,1,0:T(8,128)(2,1)} %param.16) | copy-start | bytes 1179652
  62.1 34.5 %copy-start.6 = (s32[8,8]{1,0:T(8,128)S(1)}, s32[8,8]{1,0:T(8,128)}, u32[]{:S(2)}) copy-start(s32[8,8]{1,0:T(8,128)} %param.15) | copy-start | bytes 772
  73.0 10.0 %collective-permute-start.6 = (f32[8,8,1536]{2,1,0:T(8,128)S(1)}, f32[8,8,1536]{2,1,0:T(8,128)S(1)}, u32[]{:S(2)}, u32[]{:S(2)}) collective-permute-start(f32[8,8,1536]{2,1,0:T(8,128)S(1)} %fusion.13), channel_id=1, source_target_pairs={{16,0},{20,4},{24,8},{28,12},{0,16},{4,20},{8,24},{12,28},{17,1},{... | collective-permute-start | bytes 1179656 | tf_op jit(solution)/shard_map/ppermute | solution.py:27
  85.1 34.1 %collective-permute-start = (s32[8,2]{1,0:T(8,128)S(1)}, s32[8,2]{1,0:T(8,128)S(1)}, u32[]{:S(2)}, u32[]{:S(2)}) collective-permute-start(s32[8,2]{1,0:T(8,128)S(1)} %get-tuple-element.53), channel_id=1, source_target_pairs={{0,1},{1,2},{2,3},{4,5},{5,6},{6,7},{8,9},{9,10},{10,11},{12,13},{... | collective-permute-start | bytes 200 | tf_op jit(solution)/shard_map/ppermute | solution.py:18
  89.3 29.8 %collective-permute-start.1 = (s32[8,2]{1,0:T(8,128)S(1)}, s32[8,2]{1,0:T(8,128)S(1)}, u32[]{:S(2)}, u32[]{:S(2)}) collective-permute-start(s32[8,2]{1,0:T(8,128)S(1)} %get-tuple-element.54), channel_id=1, source_target_pairs={{1,0},{2,1},{3,2},{5,4},{6,5},{7,6},{9,8},{10,9},{11,10},{13,12},{... | collective-permute-start | bytes 200 | tf_op jit(solution)/shard_map/ppermute | solution.py:19
  90.8 47.0 %collective-permute-start.2 = (bf16[8,3,2,1024]{3,2,0,1:T(2,128)(2,1)S(1)}, bf16[8,3,2,1024]{3,2,0,1:T(2,128)(2,1)S(1)}, u32[]{:S(2)}, u32[]{:S(2)}) collective-permute-start(bf16[8,3,2,1024]{3,2,0,1:T(2,128)(2,1)S(1)} %get-tuple-element.13), channel_id=1, source_target_pairs={{0,1},{1,2},{2,3},{4,5},{5,6},{6,7},{8,9},{9,10},{10,11},{12,13},{... | collective-permute-start | bytes 294920 | tf_op jit(solution)/shard_map/ppermute | solution.py:18
  95.3 42.4 %collective-permute-start.3 = (bf16[8,3,2,1024]{3,2,0,1:T(2,128)(2,1)S(1)}, bf16[8,3,2,1024]{3,2,0,1:T(2,128)(2,1)S(1)}, u32[]{:S(2)}, u32[]{:S(2)}) collective-permute-start(bf16[8,3,2,1024]{3,2,0,1:T(2,128)(2,1)S(1)} %get-tuple-element.14), channel_id=1, source_target_pairs={{1,0},{2,1},{3,2},{5,4},{6,5},{7,6},{9,8},{10,9},{11,10},{13,12},{... | collective-permute-start | bytes 294920 | tf_op jit(solution)/shard_map/ppermute | solution.py:19
  119.3 24.4 %copy-start.1 = (f32[8,1024]{1,0:T(8,128)S(1)}, f32[8,1024]{1,0:T(8,128)}, u32[]{:S(2)}) copy-start(f32[8,1024]{1,0:T(8,128)} %param.12) | copy-start | bytes 98308
  119.3 24.3 %copy-start.5 = (f32[8,1024]{1,0:T(8,128)S(1)}, f32[8,1024]{1,0:T(8,128)}, u32[]{:S(2)}) copy-start(f32[8,1024]{1,0:T(8,128)} %param.21) | copy-start | bytes 98308
  132.0 6.2 %collective-permute-start.7 = (bf16[8,2,1024]{2,1,0:T(2,128)(2,1)S(1)}, bf16[8,2,1024]{2,1,0:T(2,128)(2,1)S(1)}, u32[]{:S(2)}, u32[]{:S(2)}) collective-permute-start(bf16[8,2,1024]{2,1,0:T(2,128)(2,1)S(1)} %get-tuple-element.15), channel_id=1, source_target_pairs={{0,1},{1,2},{2,3},{4,5},{5,6},{6,7},{8,9},{9,10},{10,11},{12,13},{... | collective-permute-start | bytes 98312 | tf_op jit(solution)/shard_map/ppermute | solution.py:18
  136.4 5.8 %collective-permute-start.8 = (bf16[8,2,1024]{2,1,0:T(2,128)(2,1)S(1)}, bf16[8,2,1024]{2,1,0:T(2,128)(2,1)S(1)}, u32[]{:S(2)}, u32[]{:S(2)}) collective-permute-start(bf16[8,2,1024]{2,1,0:T(2,128)(2,1)S(1)} %get-tuple-element.16), channel_id=1, source_target_pairs={{1,0},{2,1},{3,2},{5,4},{6,5},{7,6},{9,8},{10,9},{11,10},{13,12},{... | collective-permute-start | bytes 98312 | tf_op jit(solution)/shard_map/ppermute | solution.py:19
Sparse Core Ops, SparseCore 0:
  20.8 25.0 all-gather.2
  85.1 27.6 all-gather.4
where the time goes:
time: 152 us; the launch traced here: 151 us
  local copies, waits for them, and re-layouts  67.3 us (44%)
  starting transfers between devices  25 us (16%)
  matrix products  23.4 us (15%)
  between operations  14.4 us (9%)
  waiting for transfers between devices  13.2 us (9%)
  other arithmetic  7.83 us (5%)
    gather x5, local copies, waits for them, and re-layouts, body(): footprints = jnp.take(tiles, chosen, axis=0)  61.7 us
    ppermute x4, starting transfers between devices, extended_2(): before = lax.ppermute(last, axis, up)  18.1 us
    dot_general x1, matrix products, body(): jnp.einsum('mnr,njr->mj', pieces, footprints, preferred_element_type=jnp....  12.6 us
    dot_general x1, matrix products, body(): jnp.einsum('mnj,njr->mr', pieces, footprints, preferred_element_type=jnp....  10.8 us
    ppermute x1, waiting for transfers between devices, shifted(): return lax.ppermute(block, axis, route)  8.36 us
    ppermute x4, starting transfers between devices, extended_2(): after = lax.ppermute(leading, axis, down)  5.17 us
    ppermute x4, waiting for transfers between devices, extended_2(): after = lax.ppermute(leading, axis, down)  4.8 us
  transfers between devices with their start and end apart: 11, of which 3 were waited for; matrix products, arithmetic and copies ran while one was open for 52% of the time, Pallas kernels for 0%

commit v1 on v0

v1 whole, which is shorter than its diff:
```python
import functools

import jax
import jax.numpy as jnp
from jax import lax
from jax.experimental import pallas as pl
from jax.experimental.pallas import tpu as pltpu
from jax.sharding import PartitionSpec as P

VB = 2
HALO = 2
TAPS = 3
MESH = pl.DeviceIdType.MESH
F32 = jnp.float32
BF16 = jnp.bfloat16


def kernel(
    blocks,
    slabs,
    frames,
    rows,
    volume,
    measured,
    tiles_hbm,
    tile_index,
    coefs,
    offsets,
    ray_weight,
    redundancy,
    conj_view,
    voxel_weight,
    next_ref,
    weighted_ref,
    tiles,
    gathered,
    proj,
    part_measured,
    part_weight,
    part_red,
    part_weighted,
    vol_out,
    vol_in,
    adj_out,
    adj_in,
    sib_out,
    sib_in,
    far_out,
    far_in,
    tile_sem,
    ag_send,
    ag_recv,
    fw_send,
    fw_recv,
    pt_send,
    pt_recv,
    hv_send,
    hv_recv,
    ha_send,
    ha_recv,
    sb_send,
    sb_recv,
    fr_send,
    fr_recv,
):
    me = lax.axis_index("angle")
    slab = lax.axis_index("frame")
    half = blocks // 2
    chips = blocks // 2
    core = lax.rem(me, 2)
    chip = me // 2
    sibling = me + 1 - 2 * core
    partner = lax.rem(me + half, blocks)
    count = tiles.shape[0]
    stacked = frames * rows
    sector = volume.shape[1]
    rays = measured.shape[1]
    view = rays // VB
    has_low = slab > 0
    has_high = slab < slabs - 1

    def remote(src, dst, send, recv, angle, frame=slab):
        return pltpu.make_async_remote_copy(
            src_ref=src,
            dst_ref=dst,
            send_sem=send,
            recv_sem=recv,
            device_id=(angle, frame),
            device_id_type=MESH,
        )

    def tile_copy(t):
        return pltpu.make_async_copy(tiles_hbm.at[t], tiles.at[t], tile_sem.at[t])

    for t in range(count):
        tile_copy(t).start()

    barrier = pltpu.get_barrier_semaphore()
    pl.semaphore_signal(barrier, inc=1, device_id=(sibling, slab), device_id_type=MESH)
    for d in range(1, chips):
        other = lax.rem(chip + d, chips) * 2 + core
        pl.semaphore_signal(barrier, inc=1, device_id=(other, slab), device_id_type=MESH)

    @pl.when(has_low)
    def _():
        pl.semaphore_signal(barrier, inc=1, device_id=(me, slab - 1), device_id_type=MESH)

    @pl.when(has_high)
    def _():
        pl.semaphore_signal(barrier, inc=1, device_id=(me, slab + 1), device_id_type=MESH)

    vol = volume[...]
    vol_out[0] = vol[:HALO]
    vol_out[1] = vol[rows - HALO :]

    peers = chips + has_low.astype(jnp.int32) + has_high.astype(jnp.int32)
    pl.semaphore_wait(barrier, peers)

    def halo(out, into, send, recv, side):
        return remote(
            out.at[side], into.at[1 - side], send.at[side], recv.at[1 - side], me, slab + 2 * side - 1
        )

    def exchange(out, into, send, recv):
        @pl.when(has_low)
        def _():
            halo(out, into, send, recv, 0).start()

        @pl.when(has_high)
        def _():
            halo(out, into, send, recv, 1).start()

    def exchange_wait(out, into, send, recv):
        @pl.when(has_low)
        def _():
            halo(out, into, send, recv, 0).wait_send()
            halo(out, into, send, recv, 1).wait_recv()

        @pl.when(has_high)
        def _():
            halo(out, into, send, recv, 1).wait_send()
            halo(out, into, send, recv, 0).wait_recv()

        @pl.when(slab == 0)
        def _():
            into[0] = jnp.zeros_like(into[0])

        @pl.when(slab == slabs - 1)
        def _():
            into[1] = jnp.zeros_like(into[1])

    exchange(vol_out, vol_in, hv_send, hv_recv)

    exchange_wait(vol_out, vol_in, hv_send, hv_recv)
    off = offsets[...].astype(F32)
    lane = lax.broadcasted_iota(jnp.int32, (rows, rows), 1)
    diagonal = lane == lax.broadcasted_iota(jnp.int32, (rows, rows), 0)

    def offset_column(f):
        spread = jnp.broadcast_to(off[f : f + 1, :], (rows, rows))
        return jnp.sum(jnp.where(diagonal, spread, 0.0), axis=1, keepdims=True)

    columns = [offset_column(f) for f in range(frames)]
    extended = jnp.concatenate([vol_in[0], vol, vol_in[1]], axis=0)
    sources = [extended[m : m + rows] for m in range(2 * HALO + 1)]
    group = 2 * TAPS * rows
    for p in range(frames // 2):
        taps = coefs[p * group : (p + 1) * group, :].astype(F32)
        pair = []
        for i in range(2):
            column = columns[2 * p + i]
            low = column == -2.0
            mid = column == -1.0
            total = None
            for k in range(TAPS):
                start = (i * TAPS + k) * rows
                chosen = jnp.where(
                    low, sources[k], jnp.where(mid, sources[k + 1], sources[k + 2])
                )
                term = taps[start : start + rows] * chosen
                total = term if total is None else total + term
            pair.append(total)
        gathered[me, 2 * p * rows : 2 * (p + 1) * rows, :] = jnp.concatenate(pair, axis=0).astype(
            BF16
        )

    def to_chip(d):
        target = lax.rem(chip + d, chips) * 2 + core
        return remote(gathered.at[me], gathered.at[me], ag_send.at[d], ag_recv.at[d], target)

    def from_chip(d):
        return lax.rem(chip + chips - d, chips) * 2 + core

    def to_sibling(d):
        source = from_chip(d)
        return remote(
            gathered.at[source], gathered.at[source], fw_send.at[d], fw_recv.at[d], sibling
        )

    order = sorted(range(1, chips), key=lambda d: (d != chips // 2, d))
    for d in order:
        to_chip(d).start()
    to_sibling(0).start()
    partner_copies = [
        remote(measured, part_measured, pt_send.at[0], pt_recv.at[0], partner),
        remote(ray_weight, part_weight, pt_send.at[1], pt_recv.at[1], partner),
        remote(redundancy, part_red, pt_send.at[2], pt_recv.at[2], partner),
    ]
    for copy in partner_copies:
        copy.start()
    for d in order:
        to_chip(d).wait_recv()
        to_sibling(d).start()
    for d in range(chips):
        to_sibling(d).wait_recv()

    def project(t, carry):
        tile_copy(t).wait()
        own_sector = jnp.int32(0)
        part_sector = jnp.int32(0)
        for s in range(blocks):
            own_sector = jnp.where(tile_index[me, s] == t, s, own_sector)
            part_sector = jnp.where(tile_index[partner, s] == t, s, part_sector)
        left = jnp.concatenate([gathered[own_sector], gathered[part_sector]], axis=0)
        for n in range(VB):
            span = slice(n * view, (n + 1) * view)
            proj[:, span] += jnp.dot(left, tiles[t, :, span], preferred_element_type=F32)
        return carry

    proj[...] = jnp.zeros_like(proj)
    lax.fori_loop(0, count, project, 0)

    for copy in partner_copies:
        copy.wait_recv()

    wide = 256
    flip = lax.broadcasted_iota(jnp.int32, (wide, wide), 0) + lax.broadcasted_iota(
        jnp.int32, (wide, wide), 1
    )
    flip = jnp.where(flip == wide - 1, 1.0, 0.0).astype(BF16)
    swap = conj_view[0, 0] == 1
    residuals = [
        measured[...].astype(F32) - proj[:stacked, :],
        part_measured[...].astype(F32) - proj[stacked:, :],
    ]
    mirrors = []
    for value in residuals:
        high = value.astype(BF16)
        rest = (value - high.astype(F32)).astype(BF16)
        pieces = []
        for w in range(VB):
            for u in range(view // wide):
                start = w * view + view - (u + 1) * wide
                pieces.append(
                    jnp.dot(high[:, start : start + wide], flip, preferred_element_type=F32)
                    + jnp.dot(rest[:, start : start + wide], flip, preferred_element_type=F32)
                )
        each = view // wide
        first = jnp.concatenate(pieces[:each], axis=1)
        second = jnp.concatenate(pieces[each:], axis=1)
        mirrors.append(
            jnp.concatenate(
                [jnp.where(swap, second, first), jnp.where(swap, first, second)], axis=1
            )
        )

    def combine(residual, mirrored, red, weight):
        value = red * residual + (1.0 - red) * mirrored
        return (value * jnp.concatenate([weight] * frames, axis=0)).astype(BF16)

    weighted_ref[...] = combine(residuals[0], mirrors[1], redundancy[...], ray_weight[...])
    part_weighted[...] = combine(residuals[1], mirrors[0], part_red[...], part_weight[...])

    def partial(s):
        contract = (((1,), (1,)), ((), ()))
        own = lax.dot_general(
            weighted_ref[...], tiles[tile_index[me, s]], contract, preferred_element_type=F32
        )
        other = lax.dot_general(
            part_weighted[...], tiles[tile_index[partner, s]], contract, preferred_element_type=F32
        )
        return own + other

    ring = half // 2
    side = me // half
    place = lax.rem(me, half) // 2

    def sector_at(d, c):
        return side * half + lax.rem(place + d, ring) * 2 + c

    def sib_copy(d):
        return remote(sib_out.at[d], sib_in.at[d], sb_send.at[d], sb_recv.at[d], sibling)

    def far_copy(d):
        return remote(far_out.at[d], far_in.at[d], fr_send.at[d], fr_recv.at[d], sector_at(d, core))

    for d in range(1, ring):
        sib_out[d] = partial(sector_at(d, 1 - core)).astype(BF16)
        sib_copy(d).start()
    for d in range(1, ring):
        value = partial(sector_at(d, core))
        sib_copy(d).wait_recv()
        far_out[d] = (value + sib_in[d].astype(F32)).astype(BF16)
        far_copy(d).start()
    sib_out[0] = partial(sector_at(0, 1 - core)).astype(BF16)
    sib_copy(0).start()
    image = partial(me)
    for d in range(1, ring):
        far_copy(d).wait_recv()
        image = image + far_in[d].astype(F32)
    sib_copy(0).wait_recv()
    image = image + sib_in[0].astype(F32)

    spread = [jnp.zeros((rows, sector), F32) for _ in range(2 * HALO + 1)]
    for p in range(frames // 2):
        taps = coefs[p * group : (p + 1) * group, :].astype(F32)
        for i in range(2):
            f = 2 * p + i
            column = columns[f]
            slices = image[f * rows : (f + 1) * rows]
            for k in range(TAPS):
                start = (i * TAPS + k) * rows
                term = taps[start : start + rows] * slices
                for j in range(HALO + 1):
                    spread[k + j] = spread[k + j] + jnp.where(
                        column == float(j - HALO), term, 0.0
                    )
    empty = jnp.zeros((HALO, sector), F32)
    total = None
    for m in range(2 * HALO + 1):
        parts = [jnp.zeros((m, sector), F32)] if m else []
        parts.append(spread[m])
        if m < 2 * HALO:
            parts.append(jnp.zeros((2 * HALO - m, sector), F32))
        padded = jnp.concatenate(parts, axis=0)
        total = padded if total is None else total + padded
    adj_out[0] = total[:HALO]
    adj_out[1] = total[rows + HALO :]
    exchange(adj_out, adj_in, ha_send, ha_recv)
    for d in order:
        to_chip(d).wait_send()
    for d in range(chips):
        to_sibling(d).wait_send()
    for copy in partner_copies:
        copy.wait_send()
    for d in range(ring):
        sib_copy(d).wait_send()
    for d in range(1, ring):
        far_copy(d).wait_send()
    exchange_wait(adj_out, adj_in, ha_send, ha_recv)
    middle = jnp.zeros((rows - 2 * HALO, sector), F32)
    edges = jnp.concatenate([adj_in[0], middle, adj_in[1]], axis=0)
    adjoint = total[HALO : rows + HALO] + edges
    next_ref[...] = vol + voxel_weight[...] * adjoint


def body(
    volume,
    measured,
    tiles,
    tile_index,
    warp_coef,
    warp_offset,
    ray_weight,
    redundancy,
    conj_view,
    voxel_weight,
):
    frames, rows, rays = measured.shape
    sector = volume.shape[1]
    blocks = lax.axis_size("angle")
    slabs = lax.axis_size("frame")
    stacked = frames * rows
    ring = blocks // 4
    vmem = pl.BlockSpec(memory_space=pltpu.VMEM)
    smem = pl.BlockSpec(memory_space=pltpu.SMEM)
    dma = pltpu.SemaphoreType.DMA
    flops = 8 * stacked * blocks * sector * rays
    volume_next, weighted = pl.pallas_call(
        functools.partial(kernel, blocks, slabs, frames, rows),
        out_shape=(
            jax.ShapeDtypeStruct(volume.shape, F32),
            jax.ShapeDtypeStruct((stacked, rays), BF16),
        ),
        in_specs=[
            vmem,
            vmem,
            pl.BlockSpec(memory_space=pl.ANY),
            smem,
            vmem,
            vmem,
            vmem,
            vmem,
            smem,
            vmem,
        ],
        out_specs=(vmem, vmem),
        scratch_shapes=[
            pltpu.VMEM(tiles.shape, BF16),
            pltpu.VMEM((blocks, stacked, sector), BF16),
            pltpu.VMEM((2 * stacked, rays), F32),
            pltpu.VMEM((stacked, rays), BF16),
            pltpu.VMEM(ray_weight.shape, F32),
            pltpu.VMEM((1, rays), F32),
            pltpu.VMEM((stacked, rays), BF16),
            pltpu.VMEM((2, HALO, sector), F32),
            pltpu.VMEM((2, HALO, sector), F32),
            pltpu.VMEM((2, HALO, sector), F32),
            pltpu.VMEM((2, HALO, sector), F32),
            pltpu.VMEM((ring, stacked, sector), BF16),
            pltpu.VMEM((ring, stacked, sector), BF16),
            pltpu.VMEM((ring, stacked, sector), BF16),
            pltpu.VMEM((ring, stacked, sector), BF16),
            dma((tiles.shape[0],)),
            dma((blocks // 2,)),
            dma((blocks // 2,)),
            dma((blocks // 2,)),
            dma((blocks // 2,)),
            dma((3,)),
            dma((3,)),
            dma((2,)),
            dma((2,)),
            dma((2,)),
            dma((2,)),
            dma((ring,)),
            dma((ring,)),
            dma((ring,)),
            dma((ring,)),
        ],
        cost_estimate=pl.CostEstimate(
            flops=flops, bytes_accessed=2 * tiles.size, transcendentals=0
        ),
        compiler_params=pltpu.CompilerParams(
            collective_id=0, has_side_effects=True, vmem_limit_bytes=62 * 1024 * 1024
        ),
    )(
        volume,
        measured.reshape(stacked, rays),
        tiles,
        tile_index,
        warp_coef.reshape(frames * TAPS * rows, sector),
        warp_offset,
        ray_weight,
        redundancy.reshape(1, rays),
        conj_view,
        voxel_weight,
    )
    return volume_next, weighted.reshape(frames, rows, rays)


def solution(mesh):
    placed = (
        P("frame", "angle"),
        P(None, "frame", "angle"),
        P(),
        P(),
        P(None, None, "frame", "angle"),
        P(None, "frame"),
        P("frame", "angle"),
        P("angle"),
        P("angle", None),
        P("frame", "angle"),
    )
    return jax.shard_map(
        body,
        mesh=mesh,
        in_specs=placed,
        out_specs=(P("frame", "angle"), P(None, "frame", "angle")),
        check_vma=False,
    )
```

time: 152 us -> 41.3 us (0.27)
  local copies, waits for them, and re-layouts: 67.3 us -> 4.29 us
  Pallas kernels: 0 us -> 36.1 us
  starting transfers between devices: 25 us -> 0 us
  matrix products: 23.4 us -> 0 us
  between operations: 14.4 us -> 0.64 us
  waiting for transfers between devices: 13.2 us -> 0 us
  other arithmetic: 7.83 us -> 0 us
    gather x6 -> x0, local copies, waits for them, and re-layouts: 62.3 us -> none  [the longest x5 61.7 us: body(): footprints = jnp.take(tiles, chosen, axis=0)]
    pallas_call x0 -> x1, Pallas kernels: none -> 36.1 us  [body(): pl.pallas_call(functools.partial(kernel, blocks, slabs, frames, rows), ou...]
    ppermute x9 -> x0, starting transfers between devices: 24.9 us -> none  [the longest x4 18.1 us: extended_2(): before = lax.ppermute(last, axis, up)]
    dot_general x2 -> x0, matrix products: 23.4 us -> none  [the longest x1 12.6 us: body(): jnp.einsum('mnr,njr->mj', pieces, footprints, preferred_element_type=jnp....]
    ppermute x9 -> x0, waiting for transfers between devices: 13.2 us -> none  [the longest x1 8.36 us: shifted(): return lax.ppermute(block, axis, route)]
    convert_element_type x4 -> x0, other arithmetic: 2.98 us -> none  [the longest x1 2.14 us: body(): warped = warped.astype(jnp.bfloat16).reshape(stacked, sector)]
  transfers between devices with their start and end apart: 11 -> 0, of which waited for: 3 -> 0; matrix products, arithmetic and copies ran while one was open for 52% -> 0% of each run, Pallas kernels for 0% -> 0%
where the time goes in v1:
time: 41.3 us; the launch traced here: 41 us
  Pallas kernels  36.1 us (87%)
  local copies, waits for them, and re-layouts  4.29 us (10%)
  between operations  0.64 us (2%)
    pallas_call x1, Pallas kernels, body(): pl.pallas_call(functools.partial(kernel, blocks, slabs, frames, rows), ou...  36.1 us
    unnamed x2, local copies, waits for them, and re-layouts  2.99 us
    reshape x1, local copies, waits for them, and re-layouts, body(): redundancy.reshape(1, rays)  1.29 us

profile of v1, /device:TPU:0, one launch (start us, length us, event | category | flops | bytes accessed | tf_op | source)
XLA Modules:
  0.0 41.0 jit_solution(7785167802872801694)
XLA Ops:
  0.6 1.3 %reshape.18.redundancy = f32[1,1536]{1,0:T(1,128)} reshape(f32[1536]{0:T(1024)} %param.17) | data formatting | bytes 12288 | tf_op jit(solution)/shard_map/reshape | solution.py:444
  1.9 36.1 %shard_map.113 = (f32[8,1024]{1,0:T(8,128)}, bf16[64,1536]{1,0:T(8,128)(2,1)}) custom-call(f32[8,1024]{1,0:T(8,128)} %volume.1, bf16[64,1536]{1,0:T(8,128)(2,1)} %bitcast.4, bf16[8,1024,1536]{2,1,0:T(8,128)(2,1)} %tiles_hbm.1, s32[8,8]{1,0:T(8,128)} %tile_index.1, bf16[192,1024]{1,0:T(8,128)(2,1)} %bitcast.3, s32[8,8]{1,0:T(8,128)} %offsets.1, ...), custom_call_target="tpu_custom_call" | custom-call | flops 6442450944 | bytes 25165824 | tf_op jit(solution)/shard_map/pallas_call | solution.py:379
  38.0 1.4 %copy.14 = f32[8,1024]{1,0:T(8,128)} copy(f32[8,1024]{1,0:T(8,128)} %get-tuple-element.8) | data formatting | bytes 65536
  39.4 1.6 %copy.15 = bf16[8,8,1536]{2,1,0:T(8,128)(2,1)} copy(bf16[8,8,1536]{2,1,0:T(8,128)(2,1)} %bitcast.5) | data formatting | bytes 393216

commit v2 on v1

--- a/solution.py
+++ b/solution.py
@@ -20,15 +20,23 @@
     slabs,
     frames,
     rows,
+    volume_hbm,
+    measured_hbm,
+    tiles_hbm,
+    tile_index,
+    coefs_hbm,
+    offsets,
+    weight_hbm,
+    red_hbm,
+    conj_view,
+    voxel_hbm,
+    next_hbm,
+    weighted_hbm,
     volume,
     measured,
-    tiles_hbm,
-    tile_index,
     coefs,
-    offsets,
     ray_weight,
     redundancy,
-    conj_view,
     voxel_weight,
     next_ref,
     weighted_ref,
@@ -47,6 +55,8 @@
     sib_in,
     far_out,
     far_in,
+    in_sem,
+    out_sem,
     tile_sem,
     ag_send,
     ag_recv,
@@ -92,9 +102,6 @@
     def tile_copy(t):
         return pltpu.make_async_copy(tiles_hbm.at[t], tiles.at[t], tile_sem.at[t])
 
-    for t in range(count):
-        tile_copy(t).start()
-
     barrier = pltpu.get_barrier_semaphore()
     pl.semaphore_signal(barrier, inc=1, device_id=(sibling, slab), device_id_type=MESH)
     for d in range(1, chips):
@@ -109,6 +116,22 @@
     def _():
         pl.semaphore_signal(barrier, inc=1, device_id=(me, slab + 1), device_id_type=MESH)
 
+    local = [
+        pltpu.make_async_copy(src, dst, in_sem.at[n])
+        for n, (src, dst) in enumerate(
+            (
+                (volume_hbm, volume),
+                (coefs_hbm, coefs),
+                (measured_hbm, measured),
+                (weight_hbm, ray_weight),
+                (red_hbm, redundancy),
+                (voxel_hbm, voxel_weight),
+            )
+        )
+    ]
+    for copy in local:
+        copy.start()
+    local[0].wait()
     vol = volume[...]
     vol_out[0] = vol[:HALO]
     vol_out[1] = vol[rows - HALO :]
@@ -151,7 +174,6 @@
 
     exchange(vol_out, vol_in, hv_send, hv_recv)
 
-    exchange_wait(vol_out, vol_in, hv_send, hv_recv)
     off = offsets[...].astype(F32)
     lane = lax.broadcasted_iota(jnp.int32, (rows, rows), 1)
     diagonal = lane == lax.broadcasted_iota(jnp.int32, (rows, rows), 0)
@@ -161,58 +183,103 @@
         return jnp.sum(jnp.where(diagonal, spread, 0.0), axis=1, keepdims=True)
 
     columns = [offset_column(f) for f in range(frames)]
-    extended = jnp.concatenate([vol_in[0], vol, vol_in[1]], axis=0)
-    sources = [extended[m : m + rows] for m in range(2 * HALO + 1)]
     group = 2 * TAPS * rows
-    for p in range(frames // 2):
-        taps = coefs[p * group : (p + 1) * group, :].astype(F32)
-        pair = []
-        for i in range(2):
-            column = columns[2 * p + i]
-            low = column == -2.0
-            mid = column == -1.0
-            total = None
-            for k in range(TAPS):
-                start = (i * TAPS + k) * rows
-                chosen = jnp.where(
-                    low, sources[k], jnp.where(mid, sources[k + 1], sources[k + 2])
-                )
-                term = taps[start : start + rows] * chosen
-                total = term if total is None else total + term
-            pair.append(total)
-        gathered[me, 2 * p * rows : 2 * (p + 1) * rows, :] = jnp.concatenate(pair, axis=0).astype(
-            BF16
-        )
-
-    def to_chip(d):
-        target = lax.rem(chip + d, chips) * 2 + core
-        return remote(gathered.at[me], gathered.at[me], ag_send.at[d], ag_recv.at[d], target)
-
-    def from_chip(d):
-        return lax.rem(chip + chips - d, chips) * 2 + core
-
-    def to_sibling(d):
-        source = from_chip(d)
+
+    def warp(below, above):
+        extended = jnp.concatenate([below, vol, above], axis=0)
+        sources = [extended[m : m + rows] for m in range(2 * HALO + 1)]
+        warped = []
+        for p in range(frames // 2):
+            taps = coefs[p * group : (p + 1) * group, :].astype(F32)
+            for i in range(2):
+                column = columns[2 * p + i]
+                low = column == -2.0
+                mid = column == -1.0
+                total = None
+                for k in range(TAPS):
+                    start = (i * TAPS + k) * rows
+                    chosen = jnp.where(
+                        low, sources[k], jnp.where(mid, sources[k + 1], sources[k + 2])
+                    )
+                    term = taps[start : start + rows] * chosen
+                    total = term if total is None else total + term
+                warped.append(total)
+        return warped
+
+    grid4 = chips == 4
+    across = (chip // 2) * 2 + 1 - lax.rem(chip, 2)
+    along = lax.rem(chip + chips // 2, chips)
+
+    def source(d):
+        if grid4:
+            there = (None, across, along, lax.rem(across + 2, 4))[d] if d else chip
+        else:
+            there = lax.rem(chip + chips - d, chips)
+        return there * 2 + core
+
+    def cross(d, j):
+        block, target = me, lax.rem(chip + d, chips)
+        if grid4:
+            block = source(2) if d == 3 else me
+            target = along if d == 2 else across
         return remote(
-            gathered.at[source], gathered.at[source], fw_send.at[d], fw_recv.at[d], sibling
-        )
-
-    order = sorted(range(1, chips), key=lambda d: (d != chips // 2, d))
-    for d in order:
-        to_chip(d).start()
-    to_sibling(0).start()
+            gathered.at[block, j],
+            gathered.at[block, j],
+            ag_send.at[d, j],
+            ag_recv.at[d, j],
+            target * 2 + core,
+        )
+
+    def to_sibling(d, j):
+        block = source(d)
+        return remote(
+            gathered.at[block, j],
+            gathered.at[block, j],
+            fw_send.at[d, j],
+            fw_recv.at[d, j],
+            sibling,
+        )
+
+    first = (2, 1) if grid4 else tuple(range(1, chips))
+    order = (2, 1, 3) if grid4 else first
+
+    def spread_chunk(j):
+        for d in first:
+            cross(d, j).start()
+        to_sibling(0, j).start()
+
+    def pass_chunk(j):
+        for d in order:
+            cross(d, j).wait_recv()
+            if grid4 and d == 2:
+                cross(3, j).start()
+            to_sibling(d, j).start()
+
     partner_copies = [
-        remote(measured, part_measured, pt_send.at[0], pt_recv.at[0], partner),
-        remote(ray_weight, part_weight, pt_send.at[1], pt_recv.at[1], partner),
-        remote(redundancy, part_red, pt_send.at[2], pt_recv.at[2], partner),
+        remote(measured_hbm, part_measured, pt_send.at[0], pt_recv.at[0], partner),
+        remote(weight_hbm, part_weight, pt_send.at[1], pt_recv.at[1], partner),
+        remote(red_hbm, part_red, pt_send.at[2], pt_recv.at[2], partner),
     ]
+    local[1].wait()
+    for t in range(count):
+        tile_copy(t).start()
+    outside = jnp.zeros((HALO, sector), F32)
+    inner = [value[HALO : rows - HALO] for value in warp(outside, outside)]
+    gathered[me, 0] = jnp.concatenate(inner, axis=0).astype(BF16)
+    spread_chunk(0)
+    exchange_wait(vol_out, vol_in, hv_send, hv_recv)
+    outer = []
+    for value in warp(vol_in[0], vol_in[1]):
+        outer += [value[:HALO], value[rows - HALO :]]
+    gathered[me, 1] = jnp.concatenate(outer, axis=0).astype(BF16)
+    spread_chunk(1)
     for copy in partner_copies:
         copy.start()
-    for d in order:
-        to_chip(d).wait_recv()
-        to_sibling(d).start()
-    for d in range(chips):
-        to_sibling(d).wait_recv()
+    pass_chunk(0)
+    pass_chunk(1)
+    for j in range(2):
+        for d in range(chips):
+            to_sibling(d, j).wait_recv()
 
     def project(t, carry):
         tile_copy(t).wait()
@@ -221,7 +288,13 @@
         for s in range(blocks):
             own_sector = jnp.where(tile_index[me, s] == t, s, own_sector)
             part_sector = jnp.where(tile_index[partner, s] == t, s, part_sector)
-        left = jnp.concatenate([gathered[own_sector], gathered[part_sector]], axis=0)
+        left = jnp.concatenate(
+            [
+                gathered[own_sector].reshape(stacked, sector),
+                gathered[part_sector].reshape(stacked, sector),
+            ],
+            axis=0,
+        )
         for n in range(VB):
             span = slice(n * view, (n + 1) * view)
             proj[:, span] += jnp.dot(left, tiles[t, :, span], preferred_element_type=F32)
@@ -230,8 +303,21 @@
     proj[...] = jnp.zeros_like(proj)
     lax.fori_loop(0, count, project, 0)
 
+    for copy in local[2:]:
+        copy.wait()
     for copy in partner_copies:
         copy.wait_recv()
+
+    inside = rows - 2 * HALO
+    chunk = frames * inside
+
+    def in_order(base):
+        pieces = []
+        for f in range(frames):
+            a = base + f * inside
+            b = base + chunk + f * 2 * HALO
+            pieces += [proj[b : b + HALO, :], proj[a : a + inside, :], proj[b + HALO : b + 2 * HALO, :]]
+        return jnp.concatenate(pieces, axis=0)
 
     wide = 256
     flip = lax.broadcasted_iota(jnp.int32, (wide, wide), 0) + lax.broadcasted_iota(
@@ -240,8 +326,8 @@
     flip = jnp.where(flip == wide - 1, 1.0, 0.0).astype(BF16)
     swap = conj_view[0, 0] == 1
     residuals = [
-        measured[...].astype(F32) - proj[:stacked, :],
-        part_measured[...].astype(F32) - proj[stacked:, :],
+        measured[...].astype(F32) - in_order(0),
+        part_measured[...].astype(F32) - in_order(stacked),
     ]
     mirrors = []
     for value in residuals:
@@ -256,19 +342,22 @@
                     + jnp.dot(rest[:, start : start + wide], flip, preferred_element_type=F32)
                 )
         each = view // wide
-        first = jnp.concatenate(pieces[:each], axis=1)
-        second = jnp.concatenate(pieces[each:], axis=1)
+        head = jnp.concatenate(pieces[:each], axis=1)
+        tail = jnp.concatenate(pieces[each:], axis=1)
         mirrors.append(
             jnp.concatenate(
-                [jnp.where(swap, second, first), jnp.where(swap, first, second)], axis=1
+                [jnp.where(swap, tail, head), jnp.where(swap, head, tail)], axis=1
             )
         )
 
     def combine(residual, mirrored, red, weight):
+        red = jnp.broadcast_to(red[None, :], residual.shape)
         value = red * residual + (1.0 - red) * mirrored
         return (value * jnp.concatenate([weight] * frames, axis=0)).astype(BF16)
 
     weighted_ref[...] = combine(residuals[0], mirrors[1], redundancy[...], ray_weight[...])
+    out_weighted = pltpu.make_async_copy(weighted_ref, weighted_hbm, out_sem.at[0])
+    out_weighted.start()
     part_weighted[...] = combine(residuals[1], mirrors[0], part_red[...], part_weight[...])
 
     def partial(s):
@@ -337,10 +426,12 @@
     adj_out[0] = total[:HALO]
     adj_out[1] = total[rows + HALO :]
     exchange(adj_out, adj_in, ha_send, ha_recv)
-    for d in order:
-        to_chip(d).wait_send()
-    for d in range(chips):
-        to_sibling(d).wait_send()
+    for j in range(2):
+        for d in order:
+            cross(d, j).wait_send()
+        for d in range(chips):
+            to_sibling(d, j).wait_send()
+    out_weighted.wait()
     for copy in partner_copies:
         copy.wait_send()
     for d in range(ring):
@@ -352,6 +443,14 @@
     edges = jnp.concatenate([adj_in[0], middle, adj_in[1]], axis=0)
     adjoint = total[HALO : rows + HALO] + edges
     next_ref[...] = vol + voxel_weight[...] * adjoint
+    out_next = pltpu.make_async_copy(next_ref, next_hbm, out_sem.at[1])
+    out_next.start()
+    out_next.wait()
+
+
+def settle(next_in, weighted_in, next_out, weighted_out):
+    next_out[...] = next_in[...]
+    weighted_out[...] = weighted_in[...]
 
 
 def body(
@@ -373,6 +472,7 @@
     stacked = frames * rows
     ring = blocks // 4
     vmem = pl.BlockSpec(memory_space=pltpu.VMEM)
+    hbm = pl.BlockSpec(memory_space=pl.ANY)
     smem = pl.BlockSpec(memory_space=pltpu.SMEM)
     dma = pltpu.SemaphoreType.DMA
     flops = 8 * stacked * blocks * sector * rays
@@ -382,26 +482,23 @@
             jax.ShapeDtypeStruct(volume.shape, F32),
             jax.ShapeDtypeStruct((stacked, rays), BF16),
         ),
-        in_specs=[
-            vmem,
-            vmem,
-            pl.BlockSpec(memory_space=pl.ANY),
-            smem,
-            vmem,
-            vmem,
-            vmem,
-            vmem,
-            smem,
-            vmem,
-        ],
-        out_specs=(vmem, vmem),
+        in_specs=[hbm, hbm, hbm, smem, hbm, vmem, hbm, hbm, smem, hbm],
+        out_specs=(hbm, hbm),
         scratch_shapes=[
+            pltpu.VMEM(volume.shape, F32),
+            pltpu.VMEM((stacked, rays), BF16),
+            pltpu.VMEM((frames * TAPS * rows, sector), BF16),
+            pltpu.VMEM(ray_weight.shape, F32),
+            pltpu.VMEM((rays,), F32),
+            pltpu.VMEM(voxel_weight.shape, F32),
+            pltpu.VMEM(volume.shape, F32),
+            pltpu.VMEM((stacked, rays), BF16),
             pltpu.VMEM(tiles.shape, BF16),
-            pltpu.VMEM((blocks, stacked, sector), BF16),
+            pltpu.VMEM((blocks, 2, stacked // 2, sector), BF16),
             pltpu.VMEM((2 * stacked, rays), F32),
             pltpu.VMEM((stacked, rays), BF16),
             pltpu.VMEM(ray_weight.shape, F32),
-            pltpu.VMEM((1, rays), F32),
+            pltpu.VMEM((rays,), F32),
             pltpu.VMEM((stacked, rays), BF16),
             pltpu.VMEM((2, HALO, sector), F32),
             pltpu.VMEM((2, HALO, sector), F32),
@@ -411,11 +508,13 @@
             pltpu.VMEM((ring, stacked, sector), BF16),
             pltpu.VMEM((ring, stacked, sector), BF16),
             pltpu.VMEM((ring, stacked, sector), BF16),
+            dma((6,)),
+            dma((2,)),
             dma((tiles.shape[0],)),
-            dma((blocks // 2,)),
-            dma((blocks // 2,)),
-            dma((blocks // 2,)),
-            dma((blocks // 2,)),
+            dma((blocks // 2, 2)),
+            dma((blocks // 2, 2)),
+            dma((blocks // 2, 2)),
+            dma((blocks // 2, 2)),
             dma((3,)),
             dma((3,)),
             dma((2,)),
@@ -441,10 +540,19 @@
         warp_coef.reshape(frames * TAPS * rows, sector),
         warp_offset,
         ray_weight,
-        redundancy.reshape(1, rays),
+        redundancy,
         conj_view,
         voxel_weight,
     )
+    volume_next, weighted = pl.pallas_call(
+        settle,
+        out_shape=(
+            jax.ShapeDtypeStruct(volume.shape, F32),
+            jax.ShapeDtypeStruct((stacked, rays), BF16),
+        ),
+        in_specs=[vmem, vmem],
+        out_specs=(vmem, vmem),
+    )(volume_next, weighted)
     return volume_next, weighted.reshape(frames, rows, rays)
 
 

time: 41.3 us -> 36.9 us (0.89)
  local copies, waits for them, and re-layouts: 4.29 us -> 0 us
    unnamed x2 -> x0, local copies, waits for them, and re-layouts: 2.99 us -> none
    pallas_call x1, Pallas kernels: 36.1 us -> 34.4 us  [body(): pl.pallas_call(functools.partial(kernel, blocks, slabs, frames, rows), ou...]
    pallas_call x0 -> x1, Pallas kernels: none -> 1.64 us  [body(): pl.pallas_call(settle, out_shape=(jax.ShapeDtypeStruct(volume.shape, F32)...]
    reshape x1 -> x0, local copies, waits for them, and re-layouts: 1.29 us -> none  [body(): redundancy.reshape(1, rays)]
where the time goes in v2:
time: 36.9 us; the launch traced here: 36.7 us
  Pallas kernels  36.1 us (98%)
  between operations  0.64 us (2%)
    pallas_call x1, Pallas kernels, body(): pl.pallas_call(functools.partial(kernel, blocks, slabs, frames, rows), ou...  34.4 us
    pallas_call x1, Pallas kernels, body(): pl.pallas_call(settle, out_shape=(jax.ShapeDtypeStruct(volume.shape, F32)...  1.64 us

profile of v2, /device:TPU:0, one launch (start us, length us, event | category | flops | bytes accessed | tf_op | source)
XLA Modules:
  0.0 36.7 jit_solution(17239244705619308827)
XLA Ops:
  0.6 34.4 %shard_map.113 = (f32[8,1024]{1,0:T(8,128)}, bf16[64,1536]{1,0:T(8,128)(2,1)}) custom-call(f32[8,1024]{1,0:T(8,128)} %volume_hbm.1, bf16[64,1536]{1,0:T(8,128)(2,1)} %bitcast.4, bf16[8,1024,1536]{2,1,0:T(8,128)(2,1)} %tiles_hbm.1, s32[8,8]{1,0:T(8,128)} %tile_index.1, bf16[192,1024]{1,0:T(8,128)(2,1)} %bitcast.3, s32[8,8]{1,0:T(8,128)} %offsets.1, ...), custom_call_target="tpu_custom_call" | custom-call | flops 6442450944 | bytes 25165824 | tf_op jit(solution)/shard_map/pallas_call | solution.py:479
  35.1 1.6 %shard_map.114 = (f32[8,1024]{1,0:T(8,128)}, bf16[64,1536]{1,0:T(8,128)(2,1)}) custom-call(f32[8,1024]{1,0:T(8,128)} %get-tuple-element.6.next_in, bf16[64,1536]{1,0:T(8,128)(2,1)} %get-tuple-element.7.weighted_in), custom_call_target="tpu_custom_call" | custom-call | tf_op jit(solution)/shard_map/pallas_call | solution.py:547

commit v3 on v2

--- a/solution.py
+++ b/solution.py
@@ -206,28 +206,16 @@
                 warped.append(total)
         return warped
 
-    grid4 = chips == 4
-    across = (chip // 2) * 2 + 1 - lax.rem(chip, 2)
-    along = lax.rem(chip + chips // 2, chips)
-
     def source(d):
-        if grid4:
-            there = (None, across, along, lax.rem(across + 2, 4))[d] if d else chip
-        else:
-            there = lax.rem(chip + chips - d, chips)
-        return there * 2 + core
+        return lax.rem(chip + chips - d, chips) * 2 + core
 
     def cross(d, j):
-        block, target = me, lax.rem(chip + d, chips)
-        if grid4:
-            block = source(2) if d == 3 else me
-            target = along if d == 2 else across
         return remote(
-            gathered.at[block, j],
-            gathered.at[block, j],
+            gathered.at[me, j],
+            gathered.at[me, j],
             ag_send.at[d, j],
             ag_recv.at[d, j],
-            target * 2 + core,
+            lax.rem(chip + d, chips) * 2 + core,
         )
 
     def to_sibling(d, j):
@@ -240,19 +228,16 @@
             sibling,
         )
 
-    first = (2, 1) if grid4 else tuple(range(1, chips))
-    order = (2, 1, 3) if grid4 else first
+    order = range(1, chips)
 
     def spread_chunk(j):
-        for d in first:
+        for d in order:
             cross(d, j).start()
         to_sibling(0, j).start()
 
     def pass_chunk(j):
         for d in order:
             cross(d, j).wait_recv()
-            if grid4 and d == 2:
-                cross(3, j).start()
             to_sibling(d, j).start()
 
     partner_copies = [

time: 36.9 us -> 34.9 us (0.946)
  Pallas kernels: 36.1 us -> 34.1 us
    pallas_call x1, Pallas kernels: 34.4 us -> 32.5 us  [body(): pl.pallas_call(functools.partial(kernel, blocks, slabs, frames, rows), ou...]
where the time goes in v3:
time: 34.9 us; the launch traced here: 34.8 us
  Pallas kernels  34.1 us (98%)
  between operations  0.64 us (2%)
    pallas_call x1, Pallas kernels, body(): pl.pallas_call(functools.partial(kernel, blocks, slabs, frames, rows), ou...  32.5 us
    pallas_call x1, Pallas kernels, body(): pl.pallas_call(settle, out_shape=(jax.ShapeDtypeStruct(volume.shape, F32)...  1.64 us

profile of v3, /device:TPU:0, one launch (start us, length us, event | category | flops | bytes accessed | tf_op | source)
XLA Modules:
  0.0 34.8 jit_solution(7501685225452019772)
XLA Ops:
  0.6 32.5 %shard_map.113 = (f32[8,1024]{1,0:T(8,128)}, bf16[64,1536]{1,0:T(8,128)(2,1)}) custom-call(f32[8,1024]{1,0:T(8,128)} %volume_hbm.1, bf16[64,1536]{1,0:T(8,128)(2,1)} %bitcast.4, bf16[8,1024,1536]{2,1,0:T(8,128)(2,1)} %tiles_hbm.1, s32[8,8]{1,0:T(8,128)} %tile_index.1, bf16[192,1024]{1,0:T(8,128)(2,1)} %bitcast.3, s32[8,8]{1,0:T(8,128)} %offsets.1, ...), custom_call_target="tpu_custom_call" | custom-call | flops 6442450944 | bytes 25165824 | tf_op jit(solution)/shard_map/pallas_call | solution.py:464
  33.1 1.6 %shard_map.114 = (f32[8,1024]{1,0:T(8,128)}, bf16[64,1536]{1,0:T(8,128)(2,1)}) custom-call(f32[8,1024]{1,0:T(8,128)} %get-tuple-element.6.next_in, bf16[64,1536]{1,0:T(8,128)(2,1)} %get-tuple-element.7.weighted_in), custom_call_target="tpu_custom_call" | custom-call | tf_op jit(solution)/shard_map/pallas_call | solution.py:532
